TPU v7x, 32 devices: a whole 2x2x4 slice. The times are simulated.
32 devices in a mesh: tm: 4 (over y, x), inp: 8 (over z, core).
Axes of the slice: x: 2, y: 2, z: 4, core: 2. Of those that a mesh axis runs over, the one named last changes fastest.
Arguments:
- voltages: bfloat16 [1024, 524288], P('inp', 'tm'), may hold values from -6 to 6
- coefficients: float32 [16, 8192], replicated, may hold values from -1.5 to 1.5
Outputs:
- visibilities: float32 [2, 128, 1024, 1024], P(None, ('tm', 'inp'))
All inputs are finite; a program needn't handle non-finite values.
Results may differ from a plain program's by a relative error of at most 0.0003.
Values may be sent and summed in bfloat16 or wider, within the bound.
A program may use at most 192 MiB of HBM per device.

v0:
```python
import math

import jax
import jax.numpy as jnp
from jax import lax
from jax.sharding import PartitionSpec as P

NFFT = 8192
TAPS = 16
CH = 128
CH0 = 1024


def shifted(shard, axis, by):
    count = lax.axis_size(axis)
    pairs = [(i, i + by) for i in range(count) if 0 <= i + by < count]
    return lax.ppermute(shard, axis, pairs)


def dft_table():
    samples = jnp.arange(NFFT, dtype=jnp.int32)
    channel = CH0 + jnp.arange(CH, dtype=jnp.int32)
    phase = samples[:, None] * channel[None, :] % NFFT
    angle = phase.astype(jnp.float32) * (2.0 * math.pi / NFFT)
    return jnp.concatenate([jnp.cos(angle), -jnp.sin(angle)], axis=1) * NFFT ** (-0.5)


def filter_frames(history, frames, coefficients):
    count = frames.shape[1]
    padded = jnp.concatenate([history, frames], axis=1)
    filtered = coefficients[0] * padded[:, TAPS - 1 : TAPS - 1 + count].astype(jnp.float32)
    for tap in range(1, TAPS):
        window = padded[:, TAPS - 1 - tap : TAPS - 1 - tap + count].astype(jnp.float32)
        filtered = filtered + coefficients[tap] * window
    return filtered


def transform(filtered, table):
    rows = filtered.reshape(-1, NFFT)
    return jnp.dot(rows, table, precision=lax.Precision.HIGHEST, preferred_element_type=jnp.float32)


def shards(voltages, coefficients):
    inp_count = voltages.shape[0]
    frames = voltages.reshape(inp_count, -1, NFFT)
    s_count = frames.shape[1]
    table = dft_table()
    blank = jnp.zeros((inp_count, TAPS - 1, NFFT), jnp.bfloat16)
    filtered = filter_frames(blank, frames, coefficients)
    spectra = transform(filtered, table).reshape(inp_count, s_count, 2 * CH)
    last_frames = frames[:, s_count - (TAPS - 1) :]
    carried = filter_frames(last_frames, blank, coefficients)
    carried_spec = transform(carried, table).reshape(inp_count, TAPS - 1, 2 * CH)
    arrived = shifted(carried_spec, "tm", 1)
    spectra = jnp.concatenate([spectra[:, : TAPS - 1] + arrived, spectra[:, TAPS - 1 :]], axis=1)
    outgoing = spectra.reshape(inp_count, s_count, 2, CH).transpose(2, 3, 1, 0)
    outgoing = outgoing.reshape(2, CH, 1, 1, s_count * inp_count)
    n_time = lax.axis_size("tm")
    n_input = lax.axis_size("inp")
    received = lax.all_to_all(outgoing, ("tm", "inp"), split_axis=1, concat_axis=2, tiled=True)
    received = received.reshape(2, -1, n_time, n_input, s_count * inp_count)
    owned = received.shape[1]
    gathered = received.reshape(2, owned, n_time, n_input, s_count, inp_count)
    gathered = gathered.transpose(0, 1, 2, 4, 3, 5).reshape(
        2, owned, n_time * s_count, n_input * inp_count
    )
    stacked = jnp.concatenate([gathered[0], gathered[1]], axis=1)
    vis_real = jnp.einsum(
        "csa,csb->cab",
        stacked,
        stacked,
        precision=lax.Precision.HIGHEST,
        preferred_element_type=jnp.float32,
    )
    cross = jnp.einsum(
        "csa,csb->cab",
        gathered[1],
        gathered[0],
        precision=lax.Precision.HIGHEST,
        preferred_element_type=jnp.float32,
    )
    vis_imag = cross - jnp.swapaxes(cross, 1, 2)
    return jnp.stack([vis_real, vis_imag]) / (n_time * s_count)


def solution(mesh):
    in_specs = (P("inp", "tm"), P())
    out_specs = P(None, ("tm", "inp"), None, None)
    return jax.shard_map(shards, mesh=mesh, in_specs=in_specs, out_specs=out_specs, check_vma=False)
```

profile of v0, /device:TPU:0, one launch (start us, length us, event | category | flops | bytes accessed | tf_op | source)
XLA Modules:
  0.0 518.1 jit_solution(13769877908573575123)
XLA Ops:
  0.0 3.6 fusion.150
  3.6 0.0 copy-start
  3.6 0.6 copy-done
  4.2 17.9 %fusion.141 = (f32[8192,128]{1,0:T(8,128)}, f32[8192,128]{1,0:T(8,128)}) fusion(s32[128]{0:T(128)S(1)} %iota_add_fusion), kind=kLoop, calls=%fused_computation.179 | loop fusion | flops 15728640 | bytes 8389120 | tf_op jit(solution)/shard_map/cos | solution.py:25
  22.1 23.0 %copy.32 = bf16[16,16,8,8192]{3,2,0,1:T(8,128)(2,1)} copy(bf16[16,16,8,8192]{3,2,1,0:T(8,128)(2,1)} %bitcast.61) | data formatting | bytes 67108864 | tf_op jit(solution)/shard_map/reshape | solution.py:45
  45.1 21.3 %slice.221 = bf16[128,15,8192]{2,0,1:T(8,128)(2,1)} slice(bf16[128,16,8192]{2,0,1:T(8,128)(2,1)} %bitcast.59), slice={[0:128], [1:16], [0:8192]} | slice | bytes 62914560 | tf_op jit(solution)/shard_map/slice | solution.py:51
  66.4 7.5 %fusion.166 = f32[8192,256,1]{1,0,2:T(8,128)} fusion(f32[8192,128]{1,0:T(8,128)} %get-tuple-element.24, f32[8192,128]{1,0:T(8,128)} %get-tuple-element.23), kind=kLoop, calls=%fused_computation.161.clone.clone.2 | loop fusion | flops 4194304 | bytes 16777216 | tf_op jit(solution)/shard_map/dot_general | solution.py:40
  73.8 0.0 copy-start.1
  73.8 128.7 %fusion.48 = f32[128,15,256]{2,0,1:T(8,128)} fusion(bf16[128,15,8192]{2,0,1:T(8,128)(2,1)} %slice.221, f32[8192]{0:T(1024)S(1)} %bitcast.93, f32[8192]{0:T(1024)S(1)} %bitcast.95, f32[8192]{0:T(1024)S(1)} %bitcast.67, f32[8192]{0:T(1024)S(1)} %bitcast.69, f32[8192]{0:T(1024)S(1)} %bitcast.71, f32[8192]{0:T(1024)S(1)} %bitcast.73, f32[8192]{0:T(1024)S(1)} %bitcast.75, ...), kind=kOutput, calls=%fused_computation.77 | convolution fusion | flops 49026170880 | bytes 42336256 | tf_op jit(solution)/shard_map/dot_general | solution.py:40
  202.5 6.2 %collective-permute-start = (f32[128,15,256]{2,0,1:T(8,128)}, f32[128,15,256]{2,0,1:T(8,128)}, u32[]{:S(2)}, u32[]{:S(2)}) collective-permute-start(f32[128,15,256]{2,0,1:T(8,128)} %fusion.48), channel_id=1, source_target_pairs={{0,8},{8,16},{16,24},{1,9},{9,17},{17,25},{2,10},{10,18},{18,26},{... | collective-permute-start | bytes 5898248 | tf_op jit(solution)/shard_map/ppermute | solution.py:17
  208.6 0.0 copy-done.1
  208.6 161.7 %fusion = f32[128,16,256]{2,0,1:T(8,128)S(1)} fusion(bf16[128,16,8192]{2,0,1:T(8,128)(2,1)} %bitcast.60, f32[8192]{0:T(1024)S(1)} %bitcast.94, f32[8192]{0:T(1024)S(1)} %bitcast.96, f32[8192]{0:T(1024)S(1)} %bitcast.68, f32[8192]{0:T(1024)S(1)} %bitcast.70, f32[8192]{0:T(1024)S(1)} %bitcast.72, f32[8192]{0:T(1024)S(1)} %bitcast.74, f32[8192]{0:T(1024)S(1)} %bitcast.76, ...), kind=kOutput, calls=%fused_computation.29 | convolution fusion | flops 52332331008 | bytes 44564480 | tf_op jit(solution)/shard_map/dot_general | solution.py:40
  370.4 0.0 collective-permute-done
  370.4 1.8 slice_add_fusion
  372.2 0.2 pad_maximum_fusion
  372.4 2.1 reshape.44
  374.5 4.0 copy.27
  378.5 53.9 %all_to_all.15 = f32[2,128,1,1,2048]{4,0,3,2,1:T(2,128)} all-to-all(f32[2,128,1,1,2048]{4,0,3,2,1:T(2,128)S(1)} %copy.27), channel_id=1, replica_groups=mesh['tm'=4,'inp'=8] {'tm','inp'}, dimensions={1} | all-to-all | bytes 4194304 | tf_op jit(solution)/shard_map/all_to_all | solution.py:60
  432.5 2.9 reshape.47
  435.4 0.2 copy.33
  435.6 1.1 fusion.149
  436.8 0.3 copy.22
  437.1 0.2 squeeze.8
  437.3 1.6 copy.23
  438.9 0.2 squeeze.9
  439.0 16.0 %fusion.151 = f32[4,1024,1024]{2,1,0:T(8,128)} fusion(f32[4,64,1024]{2,1,0:T(8,128)S(1)} %squeeze.9, f32[4,64,1024]{2,1,0:T(8,128)S(1)} %squeeze.8), kind=kOutput, calls=%fused_computation.192 | convolution fusion | flops 3221225472 | bytes 18874368 | tf_op jit(solution)/shard_map/csa,csb->cab/dot_general | solution.py:75
  455.0 15.9 %convolution_bitcast_fusion = f32[1,4,1024,1024]{3,2,1,0:T(8,128)} fusion(f32[4,64,1024]{2,1,0:T(8,128)S(1)} %squeeze.9, f32[4,64,1024]{2,1,0:T(8,128)S(1)} %squeeze.8), kind=kOutput, calls=%fused_computation.159 | convolution fusion | flops 6442975232 | bytes 18874368 | tf_op jit(solution)/shard_map/csa,csb->cab/dot_general | solution.py:68
  470.9 16.4 %copy.25 = f32[4,1024,1024]{1,2,0:T(8,128)} copy(f32[4,1024,1024]{2,1,0:T(8,128)} %fusion.151) | data formatting | bytes 33554432 | tf_op jit(solution)/shard_map/csa,csb->cab/dot_general | solution.py:75
  487.2 11.8 %fusion.126 = f32[1,4,1024,1024]{3,2,1,0:T(8,128)S(1)} fusion(f32[4,1024,1024]{2,1,0:T(8,128)} %fusion.151, f32[4,1024,1024]{1,2,0:T(8,128)} %copy.25), kind=kLoop, calls=%fused_computation.158 | loop fusion | flops 4194304 | bytes 50331648 | tf_op jit(solution)/shard_map/stack | solution.py:83
  499.1 19.0 %maximum_multiply_fusion = f32[2,4,1024,1024]{3,2,1,0:T(8,128)} fusion(f32[1,4,1024,1024]{3,2,1,0:T(8,128)S(1)} %fusion.126, f32[1,4,1024,1024]{3,2,1,0:T(8,128)} %convolution_bitcast_fusion), kind=kLoop, calls=%fused_computation.124 | loop fusion | flops 16777216 | bytes 67108864 | tf_op jit(solution)/shard_map/div | solution.py:83
  (3 shorter events, 0.0 us)
Async XLA Ops:
  3.6 0.6 copy-start
  73.8 134.8 %copy-start.1 = (f32[1,8192]{1,0:T(1,128)S(1)}, f32[1,8192]{1,0:T(1,128)}, u32[]{:S(2)}) copy-start(f32[1,8192]{1,0:T(1,128)} %copy-done) | copy-start | bytes 98308
  202.5 167.9 %collective-permute-start = (f32[128,15,256]{2,0,1:T(8,128)}, f32[128,15,256]{2,0,1:T(8,128)}, u32[]{:S(2)}, u32[]{:S(2)}) collective-permute-start(f32[128,15,256]{2,0,1:T(8,128)} %fusion.48), channel_id=1, source_target_pairs={{0,8},{8,16},{16,24},{1,9},{9,17},{17,25},{2,10},{10,18},{18,26},{... | collective-permute-start | bytes 5898248 | tf_op jit(solution)/shard_map/ppermute | solution.py:17
where the time goes:
time: 519 us; the launch traced here: 518 us
  matrix products  322 us (62%)
  local copies, waits for them, and re-layouts  77.4 us (15%)
  other arithmetic  58.2 us (11%)
  blocking collectives  53.9 us (10%)
  starting transfers between devices  6.16 us (1%)
    dot_general x2, matrix products, transform(): jnp.dot(rows, table, precision=lax.Precision.HIGHEST, preferred_element_t...  290 us
    all_to_all x1, blocking collectives, shards(): lax.all_to_all(outgoing, ('tm', 'inp'), split_axis=1, concat_axis=2, tile...  53.9 us
    reshape x1, local copies, waits for them, and re-layouts, shards(): frames = voltages.reshape(inp_count, -1, NFFT)  23 us
    slice x1, local copies, waits for them, and re-layouts, shards(): last_frames = frames[:, s_count - (TAPS - 1):]  21.3 us
    div x1, other arithmetic, shards(): return jnp.stack([vis_real, vis_imag]) / (n_time * s_count)  19 us
    cos x1, other arithmetic, dft_table(): jnp.cos(angle)  17.9 us
    dot_general x1, local copies, waits for them, and re-layouts, shards(): jnp.einsum('csa,csb->cab', gathered[1], gathered[0], precision=lax.Precis...  16.4 us
    dot_general x1, matrix products, shards(): jnp.einsum('csa,csb->cab', gathered[1], gathered[0], precision=lax.Precis...  16 us
  transfers between devices with their start and end apart: 1, of which 0 were waited for; matrix products, arithmetic and copies ran while one was open for 31% of the time, Pallas kernels for 0%

commit v1 on v0

--- a/solution.py
+++ b/solution.py
@@ -37,7 +37,7 @@
 
 def transform(filtered, table):
     rows = filtered.reshape(-1, NFFT)
-    return jnp.dot(rows, table, precision=lax.Precision.HIGHEST, preferred_element_type=jnp.float32)
+    return jnp.dot(rows, table, precision=lax.Precision.HIGH, preferred_element_type=jnp.float32)
 
 
 def shards(voltages, coefficients):
@@ -64,23 +64,26 @@
     gathered = gathered.transpose(0, 1, 2, 4, 3, 5).reshape(
         2, owned, n_time * s_count, n_input * inp_count
     )
-    stacked = jnp.concatenate([gathered[0], gathered[1]], axis=1)
-    vis_real = jnp.einsum(
-        "csa,csb->cab",
-        stacked,
-        stacked,
-        precision=lax.Precision.HIGHEST,
+    real_part, imag_part = gathered[0], gathered[1]
+    left = jnp.stack(
+        [
+            jnp.concatenate([real_part, imag_part], axis=1),
+            jnp.concatenate([imag_part, real_part], axis=1),
+        ]
+    )
+    right = jnp.stack(
+        [
+            jnp.concatenate([real_part, imag_part], axis=1),
+            jnp.concatenate([real_part, -imag_part], axis=1),
+        ]
+    ) / (n_time * s_count)
+    return jnp.einsum(
+        "pcsa,pcsb->pcab",
+        left,
+        right,
+        precision=lax.Precision.HIGH,
         preferred_element_type=jnp.float32,
     )
-    cross = jnp.einsum(
-        "csa,csb->cab",
-        gathered[1],
-        gathered[0],
-        precision=lax.Precision.HIGHEST,
-        preferred_element_type=jnp.float32,
-    )
-    vis_imag = cross - jnp.swapaxes(cross, 1, 2)
-    return jnp.stack([vis_real, vis_imag]) / (n_time * s_count)
 
 
 def solution(mesh):

time: 519 us -> 445 us (0.86)
  other arithmetic: 58.2 us -> 23.4 us
  matrix products: 322 us -> 301 us
  local copies, waits for them, and re-layouts: 77.4 us -> 59.8 us
    dot_general x4 -> x3, matrix products: 322 us -> 301 us  [the longest x2 284 us: transform(): jnp.dot(rows, table, precision=lax.Precision.HIGH, preferred_element_type...]
    div x1 -> x0, other arithmetic: 19 us -> none  [shards(): return jnp.stack([vis_real, vis_imag]) / (n_time * s_count)]
    dot_general x1 -> x0, local copies, waits for them, and re-layouts: 16.4 us -> none  [shards(): jnp.einsum('csa,csb->cab', gathered[1], gathered[0], precision=lax.Precis...]
    another operation x1, other arithmetic: 11.8 us -> 2.42 us  [shards(): jnp.stack([jnp.concatenate([real_part, imag_part], axis=1), jnp.concatena...]
    dot_general x1 -> x0, other arithmetic: 7.46 us -> none  [transform(): jnp.dot(rows, table, precision=lax.Precision.HIGHEST, preferred_element_t...]
  transfers between devices with their start and end apart: 1 -> 1, of which waited for: 0 -> 0; matrix products, arithmetic and copies ran while one was open for 31% -> 37% of each run, Pallas kernels for 0% -> 0%
where the time goes in v1:
time: 445 us
  matrix products  301 us (68%)
  local copies, waits for them, and re-layouts  59.8 us (13%)
  blocking collectives  54 us (12%)
  other arithmetic  23.4 us (5%)
  starting transfers between devices  6.17 us (1%)
    dot_general x2, matrix products, transform(): jnp.dot(rows, table, precision=lax.Precision.HIGH, preferred_element_type...  284 us
    all_to_all x1, blocking collectives, shards(): lax.all_to_all(outgoing, ('tm', 'inp'), split_axis=1, concat_axis=2, tile...  54 us
    reshape x1, local copies, waits for them, and re-layouts, shards(): frames = voltages.reshape(inp_count, -1, NFFT)  23 us
    slice x1, local copies, waits for them, and re-layouts, shards(): last_frames = frames[:, s_count - (TAPS - 1):]  21.3 us
    cos x1, other arithmetic, dft_table(): jnp.cos(angle)  17.9 us
    dot_general x1, matrix products, shards(): jnp.einsum('pcsa,pcsb->pcab', left, right, precision=lax.Precision.HIGH,...  17.4 us
  transfers between devices with their start and end apart: 1, of which 0 were waited for; matrix products, arithmetic and copies ran while one was open for 37% of the time, Pallas kernels for 0%

profile of v1, /device:TPU:0, one launch (start us, length us, event | category | flops | bytes accessed | tf_op | source)
XLA Modules:
  0.0 444.6 jit_solution(14974850223612313554)
XLA Ops:
  0.0 3.6 fusion.155
  3.6 0.0 copy-start
  3.6 0.6 copy-done
  4.2 17.9 %fusion.145 = (f32[8192,128]{1,0:T(8,128)}, f32[8192,128]{1,0:T(8,128)}) fusion(s32[128]{0:T(128)S(1)} %iota_add_fusion), kind=kLoop, calls=%fused_computation.184 | loop fusion | flops 15728640 | bytes 8389120 | tf_op jit(solution)/shard_map/cos | solution.py:25
  22.1 23.0 %copy.29 = bf16[16,16,8,8192]{3,2,0,1:T(8,128)(2,1)} copy(bf16[16,16,8,8192]{3,2,1,0:T(8,128)(2,1)} %bitcast.55) | data formatting | bytes 67108864 | tf_op jit(solution)/shard_map/reshape | solution.py:45
  45.1 21.3 %slice.219 = bf16[128,15,8192]{2,0,1:T(8,128)(2,1)} slice(bf16[128,16,8192]{2,0,1:T(8,128)(2,1)} %bitcast.53), slice={[0:128], [1:16], [0:8192]} | slice | bytes 62914560 | tf_op jit(solution)/shard_map/slice | solution.py:51
  66.4 0.0 copy-start.1
  66.4 121.3 %fusion.48 = f32[128,15,256]{2,0,1:T(8,128)} fusion(bf16[128,15,8192]{2,0,1:T(8,128)(2,1)} %slice.219, f32[8192]{0:T(1024)S(1)} %bitcast.87, f32[8192]{0:T(1024)S(1)} %bitcast.89, f32[8192]{0:T(1024)S(1)} %bitcast.61, f32[8192]{0:T(1024)S(1)} %bitcast.63, f32[8192]{0:T(1024)S(1)} %bitcast.65, f32[8192]{0:T(1024)S(1)} %bitcast.67, f32[8192]{0:T(1024)S(1)} %bitcast.69, ...), kind=kOutput, calls=%fused_computation.77 | convolution fusion | flops 24871174144 | bytes 42336256 | tf_op jit(solution)/shard_map/dot_general | solution.py:40
  187.6 6.2 %collective-permute-start = (f32[128,15,256]{2,0,1:T(8,128)}, f32[128,15,256]{2,0,1:T(8,128)}, u32[]{:S(2)}, u32[]{:S(2)}) collective-permute-start(f32[128,15,256]{2,0,1:T(8,128)} %fusion.48), channel_id=1, source_target_pairs={{0,8},{8,16},{16,24},{1,9},{9,17},{17,25},{2,10},{10,18},{18,26},{... | collective-permute-start | bytes 5898248 | tf_op jit(solution)/shard_map/ppermute | solution.py:17
  193.8 0.0 copy-done.1
  193.8 162.5 %fusion = f32[128,16,256]{2,0,1:T(8,128)S(1)} fusion(bf16[128,16,8192]{2,0,1:T(8,128)(2,1)} %bitcast.54, f32[8192]{0:T(1024)S(1)} %bitcast.88, f32[8192]{0:T(1024)S(1)} %bitcast.90, f32[8192]{0:T(1024)S(1)} %bitcast.62, f32[8192]{0:T(1024)S(1)} %bitcast.64, f32[8192]{0:T(1024)S(1)} %bitcast.66, f32[8192]{0:T(1024)S(1)} %bitcast.68, f32[8192]{0:T(1024)S(1)} %bitcast.70, ...), kind=kOutput, calls=%fused_computation.29 | convolution fusion | flops 26562527232 | bytes 44564480 | tf_op jit(solution)/shard_map/dot_general | solution.py:40
  356.3 0.0 collective-permute-done
  356.3 1.8 slice_add_fusion
  358.1 0.2 pad_maximum_fusion.5
  358.3 2.1 reshape.44
  360.4 4.0 copy.24
  364.4 54.0 %all_to_all.15 = f32[2,128,1,1,2048]{4,0,3,2,1:T(2,128)} all-to-all(f32[2,128,1,1,2048]{4,0,3,2,1:T(2,128)S(1)} %copy.24), channel_id=1, replica_groups=mesh['tm'=4,'inp'=8] {'tm','inp'}, dimensions={1} | all-to-all | bytes 4194304 | tf_op jit(solution)/shard_map/all_to_all | solution.py:60
  418.4 2.9 reshape.47
  421.3 0.2 copy.30
  421.5 0.2 fusion.154
  421.7 0.3 copy.21
  422.0 0.2 squeeze.7
  422.2 1.1 neg.7
  423.3 0.3 copy.20
  423.6 1.1 squeeze.6
  424.7 2.4 maximum_bitcast_fusion
  427.2 17.4 %fusion.129 = f32[2,4,1024,1024]{3,2,1,0:T(8,128)} fusion(f32[1,4,128,1024]{3,2,1,0:T(8,128)S(1)} %get-tuple-element.6, f32[1,4,128,1024]{3,2,1,0:T(8,128)S(1)} %get-tuple-element.5, f32[1,4,128,1024]{3,2,1,0:T(8,128)S(1)} %get-tuple-element.9), kind=kOutput, calls=%fused_computation.163 | convolution fusion | flops 6445596672 | bytes 39845888 | tf_op jit(solution)/shard_map/pcsa,pcsb->pcab/dot_general | solution.py:80
  (3 shorter events, 0.0 us)
Async XLA Ops:
  3.6 0.6 copy-start
  66.4 127.4 %copy-start.1 = (f32[1,8192]{1,0:T(1,128)S(1)}, f32[1,8192]{1,0:T(1,128)}, u32[]{:S(2)}) copy-start(f32[1,8192]{1,0:T(1,128)} %copy-done) | copy-start | bytes 98308
  187.6 168.7 %collective-permute-start = (f32[128,15,256]{2,0,1:T(8,128)}, f32[128,15,256]{2,0,1:T(8,128)}, u32[]{:S(2)}, u32[]{:S(2)}) collective-permute-start(f32[128,15,256]{2,0,1:T(8,128)} %fusion.48), channel_id=1, source_target_pairs={{0,8},{8,16},{16,24},{1,9},{9,17},{17,25},{2,10},{10,18},{18,26},{... | collective-permute-start | bytes 5898248 | tf_op jit(solution)/shard_map/ppermute | solution.py:17
